TPU v7x, 32 devices: a whole 2x2x4 slice. The times are simulated.
32 devices in a mesh: rep: 8 (over y, x, core), fsdp: 4 (over z).
Axes of the slice: x: 2, y: 2, z: 4, core: 2. Of those that a mesh axis runs over, the one named last changes fastest.
Arguments:
- replica_inner_weight: bfloat16 [8, 512, 16384], P('rep', 'fsdp'), may hold values from -30 to 30
- outer_weights: float32 [512, 16384], P('fsdp'), may hold values from -6 to 6
- momentum: float32 [512, 16384], P('fsdp', 'rep'), may hold values from -4 to 4
- exponents: int32 [8, 512, 128], P('rep', 'fsdp'), may hold values from 0 to 2
- levels: int32 [16], replicated, may hold values from -60 to 60, as said below
Outputs:
- inner_next: bfloat16 [8, 512, 16384], P('rep', 'fsdp')
- momentum_next: float32 [512, 16384], P('fsdp', 'rep')
- outer_next: float32 [512, 16384], P('fsdp', 'rep')
Inputs may be any that keep to these rules, and one draw needn't show every extreme that they name: `levels`: 16 distinct values, half of them negative and half positive, ascending.
All inputs are finite; a program needn't handle non-finite values. Where the computation divides by a largest or mean magnitude, that divisor is 1e-20 or more.
Results may differ from a plain program's by a relative error of at most 0.0085.
Values may be sent and summed in bfloat16 or wider, within the bound.
A program may use at most 128 MiB of HBM per device.

v0:
```python
import jax
import jax.numpy as jnp
from jax import lax
from jax.sharding import PartitionSpec as P

NLEV = 16


softness_factor = 0.02
clip_rms = 0.1
outer_rate = 0.7
outer_mu = 0.9
mix_rate = 0.5


def encode_grad(pseudo_grad, exponents, levels):
    quantize_grid_points = levels.astype(jnp.float32) / jnp.max(jnp.abs(levels)).astype(jnp.float32)
    block_scale = jnp.exp2(exponents.astype(jnp.float32))[..., None]
    row_count = pseudo_grad.shape[0]
    rescaled_gradient = pseudo_grad.reshape(row_count, exponents.shape[-1], -1) / block_scale
    closest_grid_level = (rescaled_gradient - quantize_grid_points[0]) ** 2
    for grid_level_index in range(1, NLEV):
        closest_grid_level = jnp.minimum(
            closest_grid_level, (rescaled_gradient - quantize_grid_points[grid_level_index]) ** 2
        )
    weighted = jnp.zeros_like(rescaled_gradient)
    weights_sum = jnp.zeros_like(rescaled_gradient)
    for grid_level_index in range(NLEV):
        current_weight = jnp.exp(
            -(
                (rescaled_gradient - quantize_grid_points[grid_level_index]) ** 2
                - closest_grid_level
            )
            / softness_factor
        )
        weighted = weighted + current_weight * quantize_grid_points[grid_level_index]
        weights_sum = weights_sum + current_weight
    coded = block_scale * weighted / weights_sum
    return coded.reshape(row_count, -1).astype(jnp.bfloat16)


def clip_factor(squares, entries):
    return jnp.minimum(
        jnp.float32(1.0), clip_rms / jnp.sqrt(squares / jnp.float32(entries) + 1e-06)
    )


def per_device(replica_inner_weight, outer_weights, momentum, exponents, levels):
    replicas = lax.axis_size("rep")
    row_count, columns = outer_weights.shape
    entries = row_count * lax.axis_size("fsdp") * columns
    width = momentum.shape[1]
    start = lax.axis_index("rep") * width
    coded = encode_grad(
        outer_weights - replica_inner_weight[0].astype(jnp.float32), exponents[0], levels
    )
    share = lax.psum_scatter(coded, "rep", scatter_dimension=1, tiled=True).astype(jnp.float32)
    mean_grad = share / jnp.float32(replicas)
    squares = lax.psum(jnp.sum(mean_grad * mean_grad), ("rep", "fsdp"))
    grad = clip_factor(squares, entries) * mean_grad
    momentum_next = outer_mu * momentum + grad
    outer_piece = lax.dynamic_slice_in_dim(outer_weights, start, width, 1)
    outer_next = outer_piece - outer_rate * (grad + outer_mu * momentum_next)
    outer_half = lax.all_gather(outer_next.astype(jnp.bfloat16), "rep", axis=1, tiled=True)
    mixed = mix_rate * outer_half.astype(jnp.float32) + (1.0 - mix_rate) * replica_inner_weight[
        0
    ].astype(jnp.float32)
    inner_next = mixed.astype(jnp.bfloat16)[None]
    return (inner_next, momentum_next, outer_next)


def solution(mesh):
    placed = (
        P("rep", "fsdp", None),
        P("fsdp", None),
        P("fsdp", "rep"),
        P("rep", "fsdp", None),
        P(),
    )
    return jax.shard_map(
        per_device,
        mesh=mesh,
        in_specs=placed,
        out_specs=(P("rep", "fsdp", None), P("fsdp", "rep"), P("fsdp", "rep")),
        check_vma=False,
    )
```

profile of v0, /device:TPU:0, one launch (start us, length us, event | category | flops | bytes accessed | tf_op | source)
XLA Modules:
  0.0 225.3 jit_solution(7055400887661273991)
XLA Ops:
  7.2 0.0 reduce-scatter.2.cloned.1.call-start
  7.2 1.3 abs_reduce_fusion
  9.2 0.0 copy-start
  9.2 0.8 convert_divide_fusion
  10.0 0.7 fusion.15
  10.7 0.9 exponential_bitcast_fusion
  11.6 2.3 %mul.122 = f32[128,128,128]{2,1,0:T(8,128)S(1)} broadcast(f32[128,128]{1,0:T(8,128)S(1)} %exponential_bitcast_fusion), dimensions={0,1} | broadcast | bytes 8454144 | tf_op jit(solution)/shard_map/mul | solution.py:38
  13.9 0.0 copy-done
  13.9 0.0 copy-start.1
  13.9 60.4 %fusion.4 = bf16[128,16384]{1,0:T(8,128)(2,1)} fusion(f32[128,16384]{1,0:T(8,128)} %param.6, f32[16,8,128,128]{3,2,1,0:T(8,128)S(1)} %bitcast.34, bf16[1,128,16384]{2,1,0:T(8,128)(2,1)S(1)} %copy-done, f32[]{:T(128)} %bitcast.17, f32[]{:T(128)} %bitcast.16, f32[]{:T(128)} %bitcast.15, f32[]{:T(128)} %bitcast.14, f32[]{:T(128)} %bitcast.13, f32[]{:T(128)} %bitcast.12, ...), kind=kLoop, calls=%fused_computation.7 | loop fusion | flops 308281344 | bytes 25165888 | tf_op jit(solution)/shard_map/convert_element_type | solution.py:39
  74.3 0.0 reduce-scatter.2.cloned.1.call-update
  74.3 0.0 all-gather.2.cloned.1.call-start
  74.4 54.1 %reduce-scatter.2.cloned.1.call-done = bf16[128,2048]{1,0:T(8,128)(2,1)} async-done(((bf16[128,16384]{1,0:T(8,128)(2,1)}), bf16[128,2048]{1,0:T(8,128)(2,1)}) %reduce-scatter.2.cloned.1.call-update) | async-done | bytes 524304 | tf_op jit(solution)/shard_map/reduce_scatter | solution.py:57
  128.5 1.9 fusion.11
  130.4 39.5 %psum.7 = f32[]{:T(128)} all-reduce(f32[]{:T(128)} %fusion.11), channel_id=1, replica_groups=mesh['rep'=8,'fsdp'=4] {'rep','fsdp'}, use_global_device_ids=true, to_apply=%region_3.0 | all-reduce | flops 1 | bytes 8 | tf_op jit(solution)/shard_map/psum | solution.py:59
  170.6 0.0 copy-done.1
  170.7 3.2 %fusion.12 = (bf16[128,2048]{1,0:T(8,128)(2,1)}, f32[128,2048]{1,0:T(8,128)}, f32[128,2048]{1,0:T(8,128)}) fusion(f32[]{:T(128)S(6)} %mul.142, bf16[128,2048]{1,0:T(8,128)(2,1)} %reduce-scatter.2.cloned.1.call-done, f32[128,16384]{1,0:T(8,128)} %param.6, s32[]{:T(128)S(6)} %select_n.3, f32[128,2048]{1,0:T(8,128)S(1)} %copy-done.1), kind=kLoop, calls=%fused_computation.20 | loop fusion | flops 2359296 | bytes 5242888 | tf_op jit(solution)/shard_map/convert_element_type | solution.py:64
  173.9 0.0 all-gather.2.cloned.1.call-update
  173.9 37.8 %all-gather.2.cloned.1.call-done = bf16[128,16384]{1,0:T(8,128)(2,1)} async-done(((bf16[128,2048]{1,0:T(8,128)(2,1)}), bf16[128,16384]{1,0:T(8,128)(2,1)}) %all-gather.2.cloned.1.call-update) | async-done | bytes 4194320 | tf_op jit(solution)/shard_map/all_gather | solution.py:64
  211.7 6.7 %fusion.5 = bf16[1,128,16384]{2,1,0:T(8,128)(2,1)} fusion(bf16[128,16384]{1,0:T(8,128)(2,1)} %all-gather.2.cloned.1.call-done, bf16[1,128,16384]{2,1,0:T(8,128)(2,1)} %param.5), kind=kLoop, calls=%fused_computation.8 | loop fusion | flops 10485760 | bytes 12582912 | tf_op jit(solution)/shard_map/broadcast_in_dim | solution.py:68
Async XLA Ops:
  7.2 121.3 %reduce-scatter.2.cloned.1.call-start = ((), (), s32[]{:S(2)}) async-start(), calls=%async_computation.1 | async-start | bytes 4718592 | tf_op jit(solution)/shard_map/reduce_scatter | solution.py:57
  9.2 4.7 %copy-start = (bf16[1,128,16384]{2,1,0:T(8,128)(2,1)S(1)}, bf16[1,128,16384]{2,1,0:T(8,128)(2,1)}, u32[]{:S(2)}) copy-start(bf16[1,128,16384]{2,1,0:T(8,128)(2,1)} %param.5) | copy-start | bytes 12582916
  13.9 156.8 %copy-start.1 = (f32[128,2048]{1,0:T(8,128)S(1)}, f32[128,2048]{1,0:T(8,128)}, u32[]{:S(2)}) copy-start(f32[128,2048]{1,0:T(8,128)} %param.7) | copy-start | bytes 3145732
  74.3 137.4 %all-gather.2.cloned.1.call-start = ((), (), s32[]{:S(2)}) async-start(), calls=%async_computation.2 | async-start | bytes 4718592 | tf_op jit(solution)/shard_map/all_gather | solution.py:64
Sparse Core Ops, SparseCore 0:
  74.5 53.9 reduce-scatter.1
  174.0 37.6 all-gather.1
where the time goes:
time: 226 us; the launch traced here: 225 us
  waiting for transfers between devices  91.9 us (41%)
  other arithmetic  75.2 us (33%)
  blocking collectives  39.5 us (17%)
  between operations  15.4 us (7%)
  local copies, waits for them, and re-layouts  3.03 us (1%)
    convert_element_type x1, other arithmetic, encode_grad(): return coded.reshape(row_count, -1).astype(jnp.bfloat16)  60.4 us
    reduce_scatter x1, waiting for transfers between devices, per_device(): lax.psum_scatter(coded, 'rep', scatter_dimension=1, tiled=True)  54.1 us
    psum x1, blocking collectives, per_device(): squares = lax.psum(jnp.sum(mean_grad * mean_grad), ('rep', 'fsdp'))  39.5 us
    all_gather x1, waiting for transfers between devices, per_device(): lax.all_gather(outer_next.astype(jnp.bfloat16), 'rep', axis=1, tiled=True)  37.8 us
    broadcast_in_dim x1, other arithmetic, per_device(): inner_next = mixed.astype(jnp.bfloat16)[None]  6.7 us
  transfers between devices with their start and end apart: 2, of which 2 were waited for; matrix products, arithmetic and copies ran while one was open for 0% of the time, Pallas kernels for 0%

commit v1 on v0

v1 whole, which is shorter than its diff:
```python
import functools
import math

import jax
import jax.numpy as jnp
from jax import lax
from jax.experimental import pallas as pl
from jax.experimental.pallas import tpu as pltpu
from jax.sharding import PartitionSpec as P

NLEV = 16
BLOCK = 128
ROWS_AT_ONCE = 32
CHUNKS = 4

softness_factor = 0.02
clip_rms = 0.1
outer_rate = 0.7
outer_mu = 0.9
mix_rate = 0.5

SHARP = math.sqrt(math.log2(math.e) / softness_factor)


def other_chip(q, s, chips):
    t = q
    bit = 1
    while bit < chips:
        if s & bit:
            t = t + bit * (1 - 2 * (lax.div(q, bit) % 2))
        bit *= 2
    return t


def kernel(
    reps, groups, entries,
    inner_hbm, outer_hbm, mom_hbm, expo_hbm, levels_ref,
    next_hbm, mom_next_hbm, outer_next_hbm,
    inner_v, outer_v, mom_v, expo_v, scale_v, coded_sib, coded_own, from_sib, from_chip,
    mean_v, half_v, mom_out, outer_out, parts,
    in_sem, sib_send, sib_recv, chip_send, chip_recv, part_send, part_recv,
    own_send, own_recv, fwd_send, fwd_recv, out_sem, flat_sem,
):
    chips = reps // 2
    rep = lax.axis_index("rep")
    group = lax.axis_index("fsdp")
    core = lax.rem(rep, 2)
    chip = lax.div(rep, 2)
    rows, width = mom_v.shape
    blocks = width // BLOCK
    sibling = {"rep": chip * 2 + 1 - core}
    order = list(range(chips - 1, -1, -1))
    chip_of = [other_chip(chip, s, chips) for s in range(chips)]
    peer = [{"rep": 2 * chip_of[s] + core} for s in range(chips)]
    across = [{"fsdp": lax.rem(group + s, groups)} for s in range(groups)]

    def piece(v):
        return 2 * chip_of[v // 2] + (core if v % 2 else 1 - core)

    def columns(v):
        return pl.ds(pl.multiple_of(piece(v) * width, BLOCK), width)

    expo_in = pltpu.make_async_copy(expo_hbm.at[0], expo_v, in_sem.at[2 * reps])
    expo_in.start()
    loads = {}
    for s in order:
        for v in (2 * s, 2 * s + 1):
            a = pltpu.make_async_copy(inner_hbm.at[0, :, columns(v)], inner_v.at[v], in_sem.at[2 * v])
            b = pltpu.make_async_copy(outer_hbm.at[:, columns(v)], outer_v.at[v], in_sem.at[2 * v + 1])
            a.start()
            b.start()
            loads[v] = (a, b)
    mom_in = pltpu.make_async_copy(mom_hbm, mom_v, in_sem.at[2 * reps + 1])
    mom_in.start()

    barrier = pltpu.get_barrier_semaphore()
    partners = [sibling] + peer[1:] + across[1:]
    for who in partners:
        pl.semaphore_signal(barrier, inc=1, device_id=who, device_id_type=pl.DeviceIdType.MESH)
    pl.semaphore_wait(barrier, len(partners))

    def send(src, dst, send_sem, recv_sem, who):
        copy = pltpu.make_async_remote_copy(
            src_ref=src, dst_ref=dst, send_sem=send_sem, recv_sem=recv_sem,
            device_id=who, device_id_type=pl.DeviceIdType.MESH,
        )
        copy.start()
        return copy

    most = jnp.abs(levels_ref[0])
    for k in range(1, NLEV):
        most = jnp.maximum(most, jnp.abs(levels_ref[k]))
    unit = jnp.max(SHARP / jnp.full((8, BLOCK), most.astype(jnp.float32)))
    grid = [levels_ref[k].astype(jnp.float32) * unit for k in range(NLEV)]

    expo_in.wait()
    expo = expo_v[...].astype(jnp.float32)
    scale_v[0] = jnp.exp2(expo).astype(jnp.bfloat16)
    scale_v[1] = jnp.exp2(-expo).astype(jnp.bfloat16)

    def encode(v, dst):
        first = piece(v) * blocks

        def one(b, carry):
            pick = (
                lax.broadcasted_iota(jnp.int32, (expo_v.shape[1], BLOCK), 0) == first + b
            ).astype(jnp.bfloat16)
            scale = jnp.dot(scale_v[0], pick, preferred_element_type=jnp.float32)
            inverse = jnp.dot(scale_v[1], pick, preferred_element_type=jnp.float32)
            cols = pl.ds(pl.multiple_of(b * BLOCK, BLOCK), BLOCK)
            for r in range(0, rows, ROWS_AT_ONCE):
                at = slice(r, r + ROWS_AT_ONCE)
                pseudo = outer_v[v, at, cols] - inner_v[v, at, cols].astype(jnp.float32)
                u = pseudo * (inverse[at] * SHARP)
                near = jnp.clip(u, grid[0], grid[NLEV - 1])
                far = 2.0 * u - near
                num = den = None
                for k in range(NLEV):
                    w = jnp.exp2((grid[k] - near) * (far - grid[k]))
                    num = w * grid[k] if num is None else num + w * grid[k]
                    den = w if den is None else den + w
                coded = scale[at] * (1.0 / SHARP) * num / den
                dst[at, cols] = coded.astype(jnp.bfloat16)
            return carry

        lax.fori_loop(0, blocks, one, 0)

    def over_blocks(body, init=0):
        return lax.fori_loop(
            0, blocks, lambda b, c: body(pl.ds(pl.multiple_of(b * BLOCK, BLOCK), BLOCK), c), init
        )

    f32 = jnp.float32
    pending = []
    from_sib_copies, from_chip_copies = {}, {}

    def pair_sum(s):
        from_sib_copies[s].wait_recv()
        if s == 0:
            return

        def body(cols, c):
            coded_own[s, :, cols] = (
                coded_own[s, :, cols].astype(f32) + from_sib[s, :, cols].astype(f32)
            ).astype(jnp.bfloat16)
            return c

        over_blocks(body)
        from_chip_copies[s] = send(
            coded_own.at[s], from_chip.at[s - 1], chip_send.at[s - 1], chip_recv.at[s - 1], peer[s]
        )

    for s in order:
        for v, dst in ((2 * s, coded_sib.at[s]), (2 * s + 1, coded_own.at[s])):
            for load in loads[v]:
                load.wait()
            encode(v, dst)
            if v % 2 == 0:
                from_sib_copies[s] = send(
                    coded_sib.at[s], from_sib.at[s], sib_send.at[s], sib_recv.at[s], sibling
                )
        pair_sum(s)
    for s in order[:-1]:
        from_chip_copies[s].wait_recv()

    def add_up(cols, acc):
        total = coded_own[0, :, cols].astype(f32) + from_sib[0, :, cols].astype(f32)
        for s in range(1, chips):
            total = total + from_chip[s - 1, :, cols].astype(f32)
        mean = total / f32(reps)
        mean_v[:, cols] = mean
        return acc + jnp.sum((mean * mean).reshape(rows // 8, 8, BLOCK), axis=0)

    parts[0] = over_blocks(add_up, jnp.zeros((8, BLOCK), f32))
    slot = 3
    sem = 0
    for stage, who in enumerate(([sibling], peer[1:], across[1:])):
        copies = []
        for i, one in enumerate(who):
            copies.append(
                send(parts.at[stage], parts.at[slot + i], part_send.at[sem + i], part_recv.at[sem + i], one)
            )
        total = parts[stage]
        for i, copy in enumerate(copies):
            copy.wait()
            total = total + parts[slot + i]
        slot += len(who)
        sem += len(who)
        if stage < 2:
            parts[stage + 1] = total
    squares = jnp.full((8, BLOCK), jnp.sum(total))
    clip = jnp.max(
        jnp.minimum(f32(1.0), clip_rms / jnp.sqrt(squares / f32(entries) + 1e-06))
    )

    tall = rows // CHUNKS
    mom_in.wait()
    own_copies, fwd_copies, outs = {}, {}, []

    def forward(s, c):
        v = 2 * s + 1
        at = pl.ds(c * tall, tall)
        fwd_copies[s, c] = send(
            half_v.at[v, at], half_v.at[v - 1, at],
            fwd_send.at[s * CHUNKS + c], fwd_recv.at[s * CHUNKS + c], sibling,
        )

    def mix(v, c):
        at = pl.ds(c * tall, tall)

        def body(cols, carry):
            inner_v[v, at, cols] = (
                mix_rate * half_v[v, at, cols].astype(f32)
                + (1.0 - mix_rate) * inner_v[v, at, cols].astype(f32)
            ).astype(jnp.bfloat16)
            return carry

        over_blocks(body)
        out = pltpu.make_async_copy(
            inner_v.at[v, at], next_hbm.at[0, at, columns(v)], out_sem.at[v * CHUNKS + c]
        )
        out.start()
        outs.append(out)

    for c in range(CHUNKS):
        at = pl.ds(c * tall, tall)

        def step(cols, carry):
            grad = clip * mean_v[at, cols]
            mom = outer_mu * mom_v[at, cols] + grad
            new = outer_v[1, at, cols] - outer_rate * (grad + outer_mu * mom)
            mom_out[at, cols] = mom
            outer_out[at, cols] = new
            half_v[1, at, cols] = new.astype(jnp.bfloat16)
            return carry

        over_blocks(step)
        for s in order[:-1]:
            i = (s - 1) * CHUNKS + c
            own_copies[s, c] = send(
                half_v.at[1, at], half_v.at[2 * s + 1, at], own_send.at[i], own_recv.at[i], peer[s]
            )
        forward(0, c)
    for i, (src, dst) in enumerate(((mom_out, mom_next_hbm), (outer_out, outer_next_hbm))):
        out = pltpu.make_async_copy(src, dst, flat_sem.at[i])
        out.start()
        outs.append(out)
    for c in range(CHUNKS):
        mix(1, c)
    for c in range(CHUNKS):
        fwd_copies[0, c].wait_recv()
        mix(0, c)
    last = None
    for c in range(CHUNKS):
        for s in order[-2::-1]:
            own_copies[s, c].wait_recv()
            forward(s, c)
            mix(2 * s + 1, c)
            if last is not None:
                fwd_copies[last].wait_recv()
                mix(2 * last[0], last[1])
            last = (s, c)
    if last is not None:
        fwd_copies[last].wait_recv()
        mix(2 * last[0], last[1])

    for copies in (from_sib_copies, from_chip_copies, own_copies, fwd_copies):
        for copy in copies.values():
            copy.wait_send()
    for out in outs:
        out.wait()


def per_device(inner, outer, momentum, exponents, levels):
    reps = lax.axis_size("rep")
    groups = lax.axis_size("fsdp")
    chips = reps // 2
    rows, columns = outer.shape
    width = momentum.shape[1]
    n_parts = 1 + (chips - 1) + (groups - 1)
    bf16, f32 = jnp.bfloat16, jnp.float32
    dma = pltpu.SemaphoreType.DMA
    hbm = pl.BlockSpec(memory_space=pl.ANY)
    return pl.pallas_call(
        functools.partial(kernel, reps, groups, rows * groups * columns),
        out_shape=(
            jax.ShapeDtypeStruct(inner.shape, inner.dtype),
            jax.ShapeDtypeStruct(momentum.shape, f32),
            jax.ShapeDtypeStruct(momentum.shape, f32),
        ),
        in_specs=[hbm] * 4 + [pl.BlockSpec(memory_space=pltpu.SMEM)],
        out_specs=(hbm,) * 3,
        scratch_shapes=[
            pltpu.VMEM((reps, rows, width), bf16),
            pltpu.VMEM((reps, rows, width), f32),
            pltpu.VMEM((rows, width), f32),
            pltpu.VMEM(exponents.shape[1:], jnp.int32),
            pltpu.VMEM((2,) + exponents.shape[1:], bf16),
            pltpu.VMEM((chips, rows, width), bf16),
            pltpu.VMEM((chips, rows, width), bf16),
            pltpu.VMEM((chips, rows, width), bf16),
            pltpu.VMEM((chips - 1, rows, width), bf16),
            pltpu.VMEM((rows, width), f32),
            pltpu.VMEM((reps, rows, width), bf16),
            pltpu.VMEM((rows, width), f32),
            pltpu.VMEM((rows, width), f32),
            pltpu.VMEM((3 + n_parts, 8, BLOCK), f32),
            dma((2 * reps + 2,)),
            dma((chips,)),
            dma((chips,)),
            dma((chips - 1,)),
            dma((chips - 1,)),
            dma((n_parts,)),
            dma((n_parts,)),
            dma(((chips - 1) * CHUNKS,)),
            dma(((chips - 1) * CHUNKS,)),
            dma((chips * CHUNKS,)),
            dma((chips * CHUNKS,)),
            dma((reps * CHUNKS,)),
            dma((2,)),
        ],
        compiler_params=pltpu.CompilerParams(
            collective_id=0, has_side_effects=True, vmem_limit_bytes=56 * 1024 * 1024
        ),
        cost_estimate=pl.CostEstimate(
            flops=100 * rows * columns,
            bytes_accessed=8 * rows * columns + 16 * rows * width,
            transcendentals=NLEV * rows * columns,
        ),
    )(inner, outer, momentum, exponents, levels)


def solution(mesh):
    placed = (
        P("rep", "fsdp", None),
        P("fsdp", None),
        P("fsdp", "rep"),
        P("rep", "fsdp", None),
        P(),
    )
    return jax.shard_map(
        per_device,
        mesh=mesh,
        in_specs=placed,
        out_specs=(P("rep", "fsdp", None), P("fsdp", "rep"), P("fsdp", "rep")),
        check_vma=False,
    )
```

time: 226 us -> 104 us (0.46)
  Pallas kernels: 0 us -> 96.3 us
  waiting for transfers between devices: 91.9 us -> 0 us
  other arithmetic: 75.2 us -> 0 us
  blocking collectives: 39.5 us -> 0 us
  between operations: 15.4 us -> 0.66 us
  local copies, waits for them, and re-layouts: 3.03 us -> 6.67 us
    pallas_call x0 -> x1, Pallas kernels: none -> 96.3 us  [per_device(): pl.pallas_call(functools.partial(kernel, reps, groups, rows * groups * co...]
    convert_element_type x2 -> x0, other arithmetic: 63.7 us -> none  [the longest x1 60.4 us: encode_grad(): return coded.reshape(row_count, -1).astype(jnp.bfloat16)]
    reduce_scatter x1 -> x0, waiting for transfers between devices: 54.1 us -> none  [per_device(): lax.psum_scatter(coded, 'rep', scatter_dimension=1, tiled=True)]
    psum x1 -> x0, blocking collectives: 39.5 us -> none  [per_device(): squares = lax.psum(jnp.sum(mean_grad * mean_grad), ('rep', 'fsdp'))]
    all_gather x1 -> x0, waiting for transfers between devices: 37.8 us -> none  [per_device(): lax.all_gather(outer_next.astype(jnp.bfloat16), 'rep', axis=1, tiled=True)]
    broadcast_in_dim x1 -> x0, other arithmetic: 6.7 us -> none  [per_device(): inner_next = mixed.astype(jnp.bfloat16)[None]]
    unnamed x4 -> x7, local copies, waits for them, and re-layouts: 0.01 us -> 6.67 us
    mul x1 -> x0, local copies, waits for them, and re-layouts: 2.32 us -> none  [encode_grad(): coded = block_scale * weighted / weights_sum]
  transfers between devices with their start and end apart: 2 -> 0, of which waited for: 2 -> 0; matrix products, arithmetic and copies ran while one was open for 0% -> 0% of each run, Pallas kernels for 0% -> 0%
where the time goes in v1:
time: 104 us
  Pallas kernels  96.3 us (93%)
  local copies, waits for them, and re-layouts  6.67 us (6%)
    pallas_call x1, Pallas kernels, per_device(): pl.pallas_call(functools.partial(kernel, reps, groups, rows * groups * co...  96.3 us
    unnamed x7, local copies, waits for them, and re-layouts  6.67 us

profile of v1, /device:TPU:0, one launch (start us, length us, event | category | flops | bytes accessed | tf_op | source)
XLA Modules:
  0.0 103.6 jit_solution(1153377987334063849)
XLA Ops:
  0.6 96.3 %shard_map.76 = (bf16[1,128,16384]{2,1,0:T(8,128)(2,1)}, f32[128,2048]{1,0:T(8,128)}, f32[128,2048]{1,0:T(8,128)}) custom-call(bf16[1,128,16384]{2,1,0:T(8,128)(2,1)} %inner_hbm.1, f32[128,16384]{1,0:T(8,128)} %outer_hbm.1, f32[128,2048]{1,0:T(8,128)} %mom_hbm.1, s32[1,128,128]{2,1,0:T(8,128)} %expo_hbm.1, s32[16]{0:T(128)} %levels_ref.1), custom_call_target="tpu_custom_call" | custom-call | flops 209715200 | bytes 20971520 | tf_op jit(solution)/shard_map/pallas_call | solution.py:284
  96.9 0.0 copy-start.1
  96.9 0.0 copy-start
  96.9 4.7 %copy.11 = bf16[1,128,16384]{2,1,0:T(8,128)(2,1)} copy(bf16[1,128,16384]{2,1,0:T(8,128)(2,1)} %get-tuple-element.6) | data formatting | bytes 8388608
  101.6 0.0 copy-done.1
  101.6 1.0 copy.12
  102.6 0.0 copy-done
  102.6 1.0 copy.13
Async XLA Ops:
  96.9 4.7 %copy-start.1 = (f32[128,2048]{1,0:T(8,128)S(1)}, f32[128,2048]{1,0:T(8,128)}, u32[]{:S(2)}) copy-start(f32[128,2048]{1,0:T(8,128)} %get-tuple-element.7) | copy-start | bytes 3145732
  96.9 5.7 %copy-start = (f32[128,2048]{1,0:T(8,128)S(1)}, f32[128,2048]{1,0:T(8,128)}, u32[]{:S(2)}) copy-start(f32[128,2048]{1,0:T(8,128)} %get-tuple-element.8) | copy-start | bytes 3145732

commit v2 on v1

--- a/solution.py
+++ b/solution.py
@@ -48,6 +48,7 @@
     chip = lax.div(rep, 2)
     rows, width = mom_v.shape
     blocks = width // BLOCK
+    broad = math.gcd(width, 8 * BLOCK)
     sibling = {"rep": chip * 2 + 1 - core}
     order = list(range(chips - 1, -1, -1))
     chip_of = [other_chip(chip, s, chips) for s in range(chips)]
@@ -74,7 +75,10 @@
     mom_in.start()
 
     barrier = pltpu.get_barrier_semaphore()
-    partners = [sibling] + peer[1:] + across[1:]
+    near_by = [sibling] + peer[1:] + [
+        {"rep": 2 * chip_of[s] + 1 - core} for s in range(1, chips)
+    ]
+    partners = near_by + across[1:]
     for who in partners:
         pl.semaphore_signal(barrier, inc=1, device_id=who, device_id_type=pl.DeviceIdType.MESH)
     pl.semaphore_wait(barrier, len(partners))
@@ -98,15 +102,22 @@
     scale_v[0] = jnp.exp2(expo).astype(jnp.bfloat16)
     scale_v[1] = jnp.exp2(-expo).astype(jnp.bfloat16)
 
+    f32 = jnp.float32
+
     def encode(v, dst):
         first = piece(v) * blocks
 
-        def one(b, carry):
+        def scales(b):
             pick = (
                 lax.broadcasted_iota(jnp.int32, (expo_v.shape[1], BLOCK), 0) == first + b
             ).astype(jnp.bfloat16)
-            scale = jnp.dot(scale_v[0], pick, preferred_element_type=jnp.float32)
-            inverse = jnp.dot(scale_v[1], pick, preferred_element_type=jnp.float32)
+            return tuple(
+                jnp.dot(scale_v[i], pick, preferred_element_type=jnp.float32) for i in range(2)
+            )
+
+        def one(b, carry):
+            scale, inverse = carry
+            later = scales(b + 1)
             cols = pl.ds(pl.multiple_of(b * BLOCK, BLOCK), BLOCK)
             for r in range(0, rows, ROWS_AT_ONCE):
                 at = slice(r, r + ROWS_AT_ONCE)
@@ -116,22 +127,28 @@
                 far = 2.0 * u - near
                 num = den = None
                 for k in range(NLEV):
-                    w = jnp.exp2((grid[k] - near) * (far - grid[k]))
-                    num = w * grid[k] if num is None else num + w * grid[k]
-                    den = w if den is None else den + w
-                coded = scale[at] * (1.0 / SHARP) * num / den
+                    w = jnp.exp2(((grid[k] - near) * (far - grid[k])).astype(jnp.bfloat16))
+                    wg = w * grid[k].astype(jnp.bfloat16)
+                    some_num = wg if k % 4 == 0 else some_num + wg
+                    some_den = w if k % 4 == 0 else some_den + w
+                    if k % 4 == 3:
+                        some_num, some_den = some_num.astype(f32), some_den.astype(f32)
+                        num = some_num if num is None else num + some_num
+                        den = some_den if den is None else den + some_den
+                guess = pl.reciprocal(den, approx=True)
+                guess = guess * (2.0 - den * guess)
+                coded = (scale[at] * (1.0 / SHARP)) * (num * guess)
                 dst[at, cols] = coded.astype(jnp.bfloat16)
-            return carry
-
-        lax.fori_loop(0, blocks, one, 0)
-
-    def over_blocks(body, init=0):
+            return later
+
+        lax.fori_loop(0, blocks, one, scales(0), unroll=4)
+
+    def over_blocks(body, init=0, wide=BLOCK):
         return lax.fori_loop(
-            0, blocks, lambda b, c: body(pl.ds(pl.multiple_of(b * BLOCK, BLOCK), BLOCK), c), init
+            0, width // wide, lambda b, c: body(pl.ds(pl.multiple_of(b * wide, wide), wide), c), init
         )
 
     f32 = jnp.float32
-    pending = []
     from_sib_copies, from_chip_copies = {}, {}
 
     def pair_sum(s):
@@ -145,7 +162,7 @@
             ).astype(jnp.bfloat16)
             return c
 
-        over_blocks(body)
+        over_blocks(body, wide=math.gcd(width, 2 * BLOCK))
         from_chip_copies[s] = send(
             coded_own.at[s], from_chip.at[s - 1], chip_send.at[s - 1], chip_recv.at[s - 1], peer[s]
         )
@@ -172,9 +189,9 @@
         return acc + jnp.sum((mean * mean).reshape(rows // 8, 8, BLOCK), axis=0)
 
     parts[0] = over_blocks(add_up, jnp.zeros((8, BLOCK), f32))
-    slot = 3
+    slot = 2
     sem = 0
-    for stage, who in enumerate(([sibling], peer[1:], across[1:])):
+    for stage, who in enumerate((near_by, across[1:])):
         copies = []
         for i, one in enumerate(who):
             copies.append(
@@ -186,7 +203,7 @@
             total = total + parts[slot + i]
         slot += len(who)
         sem += len(who)
-        if stage < 2:
+        if stage < 1:
             parts[stage + 1] = total
     squares = jnp.full((8, BLOCK), jnp.sum(total))
     clip = jnp.max(
@@ -194,8 +211,21 @@
     )
 
     tall = rows // CHUNKS
+    axes = [1 << i for i in range(chips.bit_length() - 1)]
     mom_in.wait()
     own_copies, fwd_copies, outs = {}, {}, []
+
+    def spread(m, c):
+        at = pl.ds(c * tall, tall)
+        for h in axes:
+            s = m | h
+            over = [bit for bit in axes if s & bit]
+            if s != m and over[c % len(over)] == h:
+                i = (s - 1) * CHUNKS + c
+                own_copies[s, c] = send(
+                    half_v.at[2 * m + 1, at], half_v.at[2 * s + 1, at],
+                    own_send.at[i], own_recv.at[i], peer[h],
+                )
 
     def forward(s, c):
         v = 2 * s + 1
@@ -215,7 +245,7 @@
             ).astype(jnp.bfloat16)
             return carry
 
-        over_blocks(body)
+        over_blocks(body, wide=broad)
         out = pltpu.make_async_copy(
             inner_v.at[v, at], next_hbm.at[0, at, columns(v)], out_sem.at[v * CHUNKS + c]
         )
@@ -234,12 +264,8 @@
             half_v[1, at, cols] = new.astype(jnp.bfloat16)
             return carry
 
-        over_blocks(step)
-        for s in order[:-1]:
-            i = (s - 1) * CHUNKS + c
-            own_copies[s, c] = send(
-                half_v.at[1, at], half_v.at[2 * s + 1, at], own_send.at[i], own_recv.at[i], peer[s]
-            )
+        over_blocks(step, wide=math.gcd(width, 4 * BLOCK))
+        spread(0, c)
         forward(0, c)
     for i, (src, dst) in enumerate(((mom_out, mom_next_hbm), (outer_out, outer_next_hbm))):
         out = pltpu.make_async_copy(src, dst, flat_sem.at[i])
@@ -251,15 +277,16 @@
         fwd_copies[0, c].wait_recv()
         mix(0, c)
     last = None
-    for c in range(CHUNKS):
-        for s in order[-2::-1]:
-            own_copies[s, c].wait_recv()
-            forward(s, c)
-            mix(2 * s + 1, c)
-            if last is not None:
-                fwd_copies[last].wait_recv()
-                mix(2 * last[0], last[1])
-            last = (s, c)
+    arrivals = [(s, c) for c in range(CHUNKS) for s in range(1, chips)]
+    for s, c in sorted(arrivals, key=lambda sc: (sc[1] + bin(sc[0]).count("1"), sc)):
+        own_copies[s, c].wait_recv()
+        spread(s, c)
+        forward(s, c)
+        mix(2 * s + 1, c)
+        if last is not None:
+            fwd_copies[last].wait_recv()
+            mix(2 * last[0], last[1])
+        last = (s, c)
     if last is not None:
         fwd_copies[last].wait_recv()
         mix(2 * last[0], last[1])
@@ -277,7 +304,7 @@
     chips = reps // 2
     rows, columns = outer.shape
     width = momentum.shape[1]
-    n_parts = 1 + (chips - 1) + (groups - 1)
+    n_parts = (reps - 1) + (groups - 1)
     bf16, f32 = jnp.bfloat16, jnp.float32
     dma = pltpu.SemaphoreType.DMA
     hbm = pl.BlockSpec(memory_space=pl.ANY)
@@ -304,7 +331,7 @@
             pltpu.VMEM((reps, rows, width), bf16),
             pltpu.VMEM((rows, width), f32),
             pltpu.VMEM((rows, width), f32),
-            pltpu.VMEM((3 + n_parts, 8, BLOCK), f32),
+            pltpu.VMEM((2 + n_parts, 8, BLOCK), f32),
             dma((2 * reps + 2,)),
             dma((chips,)),
             dma((chips,)),

time: 104 us -> 87 us (0.84)
  Pallas kernels: 96.3 us -> 79 us
    pallas_call x1, Pallas kernels: 96.3 us -> 79 us  [per_device(): pl.pallas_call(functools.partial(kernel, reps, groups, rows * groups * co...]
where the time goes in v2:
time: 87 us; the launch traced here: 86.3 us
  Pallas kernels  79 us (91%)
  local copies, waits for them, and re-layouts  6.67 us (8%)
    pallas_call x1, Pallas kernels, per_device(): pl.pallas_call(functools.partial(kernel, reps, groups, rows * groups * co...  79 us
    unnamed x7, local copies, waits for them, and re-layouts  6.67 us

profile of v2, /device:TPU:0, one launch (start us, length us, event | category | flops | bytes accessed | tf_op | source)
XLA Modules:
  0.0 86.3 jit_solution(6109818587295904767)
XLA Ops:
  0.6 79.0 %shard_map.76 = (bf16[1,128,16384]{2,1,0:T(8,128)(2,1)}, f32[128,2048]{1,0:T(8,128)}, f32[128,2048]{1,0:T(8,128)}) custom-call(bf16[1,128,16384]{2,1,0:T(8,128)(2,1)} %inner_hbm.1, f32[128,16384]{1,0:T(8,128)} %outer_hbm.1, f32[128,2048]{1,0:T(8,128)} %mom_hbm.1, s32[1,128,128]{2,1,0:T(8,128)} %expo_hbm.1, s32[16]{0:T(128)} %levels_ref.1), custom_call_target="tpu_custom_call" | custom-call | flops 209715200 | bytes 20971520 | tf_op jit(solution)/shard_map/pallas_call | solution.py:311
  79.6 0.0 copy-start.1
  79.6 0.0 copy-start
  79.6 4.7 %copy.11 = bf16[1,128,16384]{2,1,0:T(8,128)(2,1)} copy(bf16[1,128,16384]{2,1,0:T(8,128)(2,1)} %get-tuple-element.6) | data formatting | bytes 8388608
  84.4 0.0 copy-done.1
  84.4 1.0 %copy.12 = f32[128,2048]{1,0:T(8,128)} copy(f32[128,2048]{1,0:T(8,128)S(1)} %copy-done.1) | data formatting | bytes 2097152
  85.3 0.0 copy-done
  85.3 1.0 %copy.13 = f32[128,2048]{1,0:T(8,128)} copy(f32[128,2048]{1,0:T(8,128)S(1)} %copy-done) | data formatting | bytes 2097152
Async XLA Ops:
  79.6 4.7 %copy-start.1 = (f32[128,2048]{1,0:T(8,128)S(1)}, f32[128,2048]{1,0:T(8,128)}, u32[]{:S(2)}) copy-start(f32[128,2048]{1,0:T(8,128)} %get-tuple-element.7) | copy-start | bytes 3145732
  79.6 5.7 %copy-start = (f32[128,2048]{1,0:T(8,128)S(1)}, f32[128,2048]{1,0:T(8,128)}, u32[]{:S(2)}) copy-start(f32[128,2048]{1,0:T(8,128)} %get-tuple-element.8) | copy-start | bytes 3145732
